TPU v7x, 256 devices: a whole 4x4x8 slice. The times are simulated.
256 devices in a mesh: pairs: 64 (over z, y, core), quad: 4 (over x).
Axes of the slice: x: 4, y: 4, z: 8, core: 2. Of those that a mesh axis runs over, the one named last changes fastest.
Arguments:
- picture_descriptors: bfloat16 [1024, 2048, 256], P('pairs', 'quad'), may hold values from -80 to 80
- image_slot: int32 [1024], replicated, may hold values from 0 to 1023, as said below
- group_images: int32 [640], P('pairs'), may hold values from 0 to 1023, as said below
- pair_target: int32 [128], P('pairs'), may hold values from 0 to 7
- pair_count: int32 [64], P('pairs'), may hold values from 1 to 2, 80 in all
Outputs:
- correspondence_result: float32 [128, 3, 2048], P('pairs', None, 'quad')
Inputs may be any that keep to these rules, and one draw needn't show every extreme that they name: A permutation; image i is stored in row image_slot[i], on the devices of pairs index image_slot[i] div 16. `group_images`: entries g * 10 to g * 10 + 9 are the distinct images of group g, its 8 reference images first, then its 2 query images; at most 1 images of one group are stored on one pairs index, and in every group some pairs index stores exactly 1 of them. Group g uses its pairs 0 to pair_count[g] - 1.
All inputs are finite; a program needn't handle non-finite values.
Results may differ from a plain program's by a relative error of at most 0.00035.
Values may be sent and summed in bfloat16 or wider, within the bound.
No kernel may reach another device: no remote copies, remote signals or barrier semaphores. Data moves between devices by JAX's collectives and lax.ppermute only.
A program may use at most 128 MiB of HBM per device.

v0:
```python
import functools

import jax
import jax.numpy as jnp
from jax import lax
from jax.experimental import pallas as pl
from jax.experimental.pallas import tpu as pltpu
from jax.sharding import Mesh
from jax.sharding import PartitionSpec as P

IMG_W = 64
TGT_G = 8
SHARPNESS_DIVISOR = 0.1
LANES = 128
CORES = 2
PLACE_BITS = 6
PLACES = 1 << PLACE_BITS
CAPACITIES = (6, 7, 8, 9, 10, 11, 12, 16)
ANY = pl.BlockSpec(memory_space=pl.ANY)
SMEM = pl.BlockSpec(memory_space=pltpu.SMEM)
VMEM = pl.BlockSpec(memory_space=pltpu.VMEM)


def announce_kernel(pairs, image_slot, group_images, pair_target, pair_count, out):
    lane = lax.broadcasted_iota(jnp.int32, out.shape, 2)
    message = jnp.full(out.shape, -1, jnp.int32)
    for entry in range(2 * pairs):
        pair = entry % pairs
        member = TGT_G + pair if entry < pairs else pair_target[pair]
        stored = jnp.where(pair < pair_count[0], image_slot[group_images[member]], -1)
        message = jnp.where(lane == entry, stored, message)
    out[...] = message


def announce(groups, image_slot, group_images, pair_target, pair_count):
    return pl.pallas_call(
        functools.partial(announce_kernel, pair_target.shape[0]),
        in_specs=[SMEM] * 4,
        out_specs=VMEM,
        out_shape=jax.ShapeDtypeStruct((groups, 1, LANES), jnp.int32),
    )(image_slot, group_images, pair_target, pair_count)


def plan_kernel(chip_rows, entries, capacities, chip, asked, places, rows, branch):
    groups = asked.shape[0]
    table = asked[...].T
    chips_of, rows_of, stored_of = [], [], []
    wide = lax.broadcasted_iota(jnp.int32, (chip_rows, groups), 0)
    count = jnp.zeros((chip_rows, chip_rows), jnp.float32)
    for entry in range(entries):
        stored = table[entry : entry + 1, :]
        valid = jnp.where(stored >= 0, 1.0, 0.0)
        stored_of.append(jnp.maximum(stored, 0))
        chips_of.append(jnp.where(lax.div(stored_of[-1], chip_rows) == wide, valid, 0.0))
        rows_of.append(jnp.where(lax.rem(stored_of[-1], chip_rows) == wide, 1.0, 0.0))
        count += lax.dot_general(
            rows_of[-1], chips_of[-1], (((1,), (1,)), ((), ())), preferred_element_type=jnp.float32
        )
    flags = jnp.where(count > 0.0, 1.0, 0.0)
    first = lax.broadcasted_iota(jnp.int32, (chip_rows, chip_rows), 0)
    second = lax.broadcasted_iota(jnp.int32, (chip_rows, chip_rows), 1)
    earlier = jnp.dot(jnp.where(second < first, 1.0, 0.0), flags, preferred_element_type=jnp.float32)
    most = jnp.max(earlier + flags)
    choice = jnp.int32(0)
    for capacity in capacities[:-1]:
        choice += jnp.where(most > capacity, 1, 0)
    branch[0] = choice

    here = second == chip[0]
    my_flag = jnp.max(jnp.where(here, flags, 0.0), axis=1, keepdims=True)
    my_place = jnp.max(jnp.where(here, earlier, 0.0), axis=1, keepdims=True)
    slot = lax.broadcasted_iota(jnp.int32, (chip_rows, LANES), 1).astype(jnp.float32)
    row = lax.broadcasted_iota(jnp.int32, (chip_rows, LANES), 0).astype(jnp.float32)
    chosen = jnp.where((my_flag > 0.0) & (my_place == slot), row, 0.0)
    rows[...] = jnp.broadcast_to(jnp.sum(chosen, axis=0, keepdims=True), rows.shape).astype(jnp.int32)

    places[...] = earlier


def locate_kernel(chip_rows, entries, places, asked, index):
    groups = asked.shape[0]
    table = asked[...].T
    wide = lax.broadcasted_iota(jnp.int32, (chip_rows, groups), 0)
    for entry in range(entries):
        stored = jnp.maximum(table[entry : entry + 1, :], 0)
        chip = lax.div(stored, chip_rows)
        by_chip = jnp.dot(places[...], jnp.where(chip == wide, 1.0, 0.0), preferred_element_type=jnp.float32)
        place = jnp.sum(jnp.where(lax.rem(stored, chip_rows) == wide, by_chip, 0.0), axis=0, keepdims=True)
        valid = table[entry : entry + 1, :] >= 0
        index[entry : entry + 1, :] = chip * PLACES + jnp.where(valid, place.astype(jnp.int32), 0)


def locate(chip_rows, entries, places, asked):
    return pl.pallas_call(
        functools.partial(locate_kernel, chip_rows, entries),
        in_specs=[VMEM, VMEM],
        out_specs=VMEM,
        out_shape=jax.ShapeDtypeStruct((8, asked.shape[0]), jnp.int32),
    )(places, asked)


def plan(chip_rows, entries, capacities, chip, asked):
    return pl.pallas_call(
        functools.partial(plan_kernel, chip_rows, entries, capacities),
        in_specs=[SMEM, VMEM],
        out_specs=(VMEM, VMEM, SMEM),
        out_shape=(
            jax.ShapeDtypeStruct((chip_rows, chip_rows), jnp.float32),
            jax.ShapeDtypeStruct((8, LANES), jnp.int32),
            jax.ShapeDtypeStruct((1,), jnp.int32),
        ),
    )(chip, asked)


def pick_kernel(core, rows, own, other, out, sems):
    images_dev = own.shape[0]
    capacity = out.shape[1]
    for slot in range(capacity):
        row = rows[0, slot]
        local = lax.rem(row, images_dev)
        is_own = lax.div(row, images_dev) == core[0]

        @pl.when(is_own)
        def _():
            pltpu.make_async_copy(own.at[local, core[0]], out.at[:, slot], sems.at[slot]).start()

        @pl.when(jnp.logical_not(is_own))
        def _():
            pltpu.make_async_copy(other.at[local, core[0]], out.at[:, slot], sems.at[slot]).start()

    for slot in range(capacity):
        pltpu.make_async_copy(other.at[0, 0], out.at[:, slot], sems.at[slot]).wait()


def pick(capacity, core, rows, own, other):
    _, _, chips, piece, width = other.shape
    return pl.pallas_call(
        pick_kernel,
        in_specs=[SMEM, SMEM, ANY, ANY],
        out_specs=VMEM,
        out_shape=jax.ShapeDtypeStruct((chips, capacity, piece, width), other.dtype),
        scratch_shapes=[pltpu.SemaphoreType.DMA((capacity,))],
        compiler_params=pltpu.CompilerParams(vmem_limit_bytes=24 * 1024 * 1024),
    )(core, rows, own, other)


def regroup_kernel(index, spread, out):
    groups, entries = out.shape[:2]

    def step(group, carry):
        for entry in range(entries):
            code = index[entry, group]
            out[group, entry] = spread[code >> PLACE_BITS, code & (PLACES - 1)]
        return carry

    lax.fori_loop(0, groups, step, 0, unroll=16)


def regroup(groups, entries, index, spread):
    return pl.pallas_call(
        regroup_kernel,
        in_specs=[SMEM, VMEM],
        out_specs=VMEM,
        out_shape=jax.ShapeDtypeStruct((groups, entries, *spread.shape[2:]), spread.dtype),
        compiler_params=pltpu.CompilerParams(vmem_limit_bytes=24 * 1024 * 1024),
    )(index, spread)


def score_kernel(image_rows, multiplier, pair, meta, maps, near_query, near_target, *refs):
    *earlier, products, rows, columns, scores, stats = refs
    for previous in earlier:
        columns[0:pair] = previous[...]
    chips, cores, entries, piece, width = maps.shape
    part = chips * piece
    slab = cores * part
    targets = ((maps, entries // 2 + pair), (near_target, 0))
    queries = ((maps, pair), (near_query, 0))

    @pl.when(pair < meta[1])
    def _():
        for row in range(2 * cores):
            target, entry = targets[row // cores]
            tokens = target[:, row % cores, entry].reshape(part, width)
            for column in range(2 * cores):
                query, entry = queries[column // cores]
                scores[row * part : (row + 1) * part, column * part : (column + 1) * part] = (
                    lax.dot_general(
                        tokens, query[:, column % cores, entry].reshape(part, width), (((1,), (1,)), ((), ())),
                        preferred_element_type=jnp.float32,
                    )
                    * multiplier
                )

        first_lane = lax.broadcasted_iota(jnp.int32, (64, LANES), 1) == 0

        def rows_step(index, carry):
            block = pl.ds(pl.multiple_of(index * 64, 64), 64)
            top = jnp.max(scores[block, :], axis=1, keepdims=True)
            powers = jnp.exp(scores[block, :] - top)
            products[block, :] = powers
            stats[block, :] = jnp.where(first_lane, top, jnp.sum(powers, axis=1, keepdims=True))
            return carry

        lax.fori_loop(0, 2 * slab // 64, rows_step, 0, unroll=16)
        for start in range(0, 2 * slab, LANES):
            columns[pair, :, start : start + LANES] = stats[start : start + LANES, :].T[0:8, :]

        bands = slab // IMG_W
        along = lax.broadcasted_iota(jnp.int32, (IMG_W, LANES), 0).astype(jnp.float32)
        coord_x = (2.0 * along + 1.0) / IMG_W - 1.0

        def lanes_step(index, carry):
            lanes = pl.ds(pl.multiple_of(index * LANES, LANES), LANES)
            top = jnp.max(scores[:, lanes], axis=0, keepdims=True)
            total = jnp.zeros((8, LANES), jnp.float32)
            weighted_y = jnp.zeros((8, LANES), jnp.float32)
            folded = jnp.zeros((IMG_W, LANES), jnp.float32)
            for band in range(2 * bands):
                block = slice(band * IMG_W, (band + 1) * IMG_W)
                powers = jnp.exp(scores[block, lanes] - top)
                products[block, lanes] *= powers
                folded += powers
                sums = jnp.sum(powers.reshape(IMG_W // 8, 8, LANES), axis=0)
                total += sums
                image_row = meta[2 + band // bands] * bands + band % bands
                weighted_y += sums * ((2.0 * image_row.astype(jnp.float32) + 1.0) / image_rows - 1.0)
            rows[0:1, lanes] = top
            rows[1:2, lanes] = jnp.sum(total, axis=0, keepdims=True)
            rows[2:3, lanes] = jnp.sum(folded * coord_x, axis=0, keepdims=True)
            rows[3:4, lanes] = jnp.sum(weighted_y, axis=0, keepdims=True)
            return carry

        lax.fori_loop(0, 2 * slab // LANES, lanes_step, 0, unroll=8)


def score(image_rows, multiplier, pair, meta, maps, near_query, near_target, earlier):
    chips, cores, _, piece, width = maps.shape
    tokens = 2 * chips * cores * piece
    return pl.pallas_call(
        functools.partial(score_kernel, image_rows, multiplier, pair),
        in_specs=[SMEM] + [VMEM] * (3 + len(earlier)),
        out_specs=[VMEM] * 3,
        out_shape=[
            jax.ShapeDtypeStruct((tokens, tokens), jnp.float32),
            jax.ShapeDtypeStruct((8, tokens), jnp.float32),
            jax.ShapeDtypeStruct((pair + 1, 8, tokens), jnp.float32),
        ],
        scratch_shapes=[pltpu.VMEM((tokens, tokens), jnp.float32), pltpu.VMEM((tokens, LANES), jnp.float32)],
        compiler_params=pltpu.CompilerParams(vmem_limit_bytes=20 * 1024 * 1024),
        cost_estimate=pl.CostEstimate(
            flops=2 * tokens * tokens * width, bytes_accessed=2 << 20, transcendentals=2 << 20
        ),
    )(meta, maps, near_query, near_target, *earlier)


def columns_kernel(multiplier, pair, meta, maps, near_query, near_target, *refs):
    *earlier, scores, powers, columns, stats = refs
    for previous in earlier:
        columns[0:pair] = previous[...]
    chips, cores, entries, piece, width = maps.shape
    part = chips * piece
    slab = cores * part
    targets = ((maps, entries // 2 + pair), (near_target, 0))
    queries = ((maps, pair), (near_query, 0))

    @pl.when(pair < meta[1])
    def _():
        for row in range(2 * cores):
            target, entry = targets[row // cores]
            tokens = target[:, row % cores, entry].reshape(part, width)
            for column in range(2 * cores):
                query, entry = queries[column // cores]
                scores[row * part : (row + 1) * part, column * part : (column + 1) * part] = (
                    lax.dot_general(
                        tokens, query[:, column % cores, entry].reshape(part, width), (((1,), (1,)), ((), ())),
                        preferred_element_type=jnp.float32,
                    )
                    * multiplier
                )

        first_lane = lax.broadcasted_iota(jnp.int32, (64, LANES), 1) == 0
        for start in range(0, 2 * slab, 64):
            block = slice(start, start + 64)
            top = jnp.max(scores[block, :], axis=1, keepdims=True)
            exponentials = jnp.exp(scores[block, :] - top)
            powers[block, :] = exponentials
            stats[block, :] = jnp.where(first_lane, top, jnp.sum(exponentials, axis=1, keepdims=True))
        for start in range(0, 2 * slab, LANES):
            columns[pair, :, start : start + LANES] = stats[start : start + LANES, :].T[0:8, :]


def score_columns(multiplier, pair, meta, maps, near_query, near_target, earlier):
    chips, cores, _, piece, width = maps.shape
    tokens = 2 * chips * cores * piece
    square = jax.ShapeDtypeStruct((tokens, tokens), jnp.float32)
    return pl.pallas_call(
        functools.partial(columns_kernel, multiplier, pair),
        in_specs=[SMEM] + [VMEM] * (3 + len(earlier)),
        out_specs=[VMEM] * 3,
        out_shape=[square, square, jax.ShapeDtypeStruct((pair + 1, 8, tokens), jnp.float32)],
        scratch_shapes=[pltpu.VMEM((tokens, LANES), jnp.float32)],
        compiler_params=pltpu.CompilerParams(vmem_limit_bytes=16 * 1024 * 1024),
        cost_estimate=pl.CostEstimate(
            flops=2 * tokens * tokens * width, bytes_accessed=2 << 20, transcendentals=1 << 20
        ),
    )(meta, maps, near_query, near_target, *earlier)


def rows_kernel(image_rows, pair, meta, scores, powers, products, rows):
    tokens = scores.shape[0]
    bands = tokens // (2 * IMG_W)

    @pl.when(pair < meta[1])
    def _():
        along = lax.broadcasted_iota(jnp.int32, (IMG_W, LANES), 0).astype(jnp.float32)
        coord_x = (2.0 * along + 1.0) / IMG_W - 1.0
        for start in range(0, tokens, LANES):
            lanes = slice(start, start + LANES)
            top = jnp.max(scores[:, lanes], axis=0, keepdims=True)
            total = jnp.zeros((8, LANES), jnp.float32)
            weighted_y = jnp.zeros((8, LANES), jnp.float32)
            folded = jnp.zeros((IMG_W, LANES), jnp.float32)
            for band in range(2 * bands):
                block = slice(band * IMG_W, (band + 1) * IMG_W)
                exponentials = jnp.exp(scores[block, lanes] - top)
                products[block, lanes] = powers[block, lanes] * exponentials
                folded += exponentials
                sums = jnp.sum(exponentials.reshape(IMG_W // 8, 8, LANES), axis=0)
                total += sums
                image_row = meta[2 + band // bands] * bands + band % bands
                weighted_y += sums * ((2.0 * image_row.astype(jnp.float32) + 1.0) / image_rows - 1.0)
            rows[0:1, lanes] = top
            rows[1:2, lanes] = jnp.sum(total, axis=0, keepdims=True)
            rows[2:3, lanes] = jnp.sum(folded * coord_x, axis=0, keepdims=True)
            rows[3:4, lanes] = jnp.sum(weighted_y, axis=0, keepdims=True)


def score_rows(image_rows, pair, meta, scores, powers):
    tokens = scores.shape[0]
    return pl.pallas_call(
        functools.partial(rows_kernel, image_rows, pair),
        in_specs=[SMEM] + [VMEM] * 2,
        out_specs=[VMEM] * 2,
        out_shape=[
            jax.ShapeDtypeStruct((tokens, tokens), jnp.float32),
            jax.ShapeDtypeStruct((8, tokens), jnp.float32),
        ],
        compiler_params=pltpu.CompilerParams(vmem_limit_bytes=16 * 1024 * 1024),
        cost_estimate=pl.CostEstimate(flops=10 << 20, bytes_accessed=8 << 20, transcendentals=1 << 20),
    )(meta, scores, powers)


def mutual_kernel(pairs, meta, *refs):
    products, rows = refs[:pairs], refs[pairs : 2 * pairs]
    columns, others, kept, sent, weights = refs[2 * pairs :]
    tokens = weights.shape[0]
    slab = tokens // 2
    for pair in range(pairs):

        @pl.when(pair < meta[1])
        def _():
            for start in range(0, tokens, LANES):
                here = slice(start, start + LANES)
                there = slice((start + slab) % tokens, (start + slab) % tokens + LANES)
                top = columns[pair, 0:1, here]
                other_top = others[pair, 0:1, there]
                highest = jnp.maximum(top, other_top)
                scale = jnp.exp(top - highest)
                total = columns[pair, 1:2, here] * scale + others[pair, 1:2, there] * jnp.exp(other_top - highest)
                weights[here, :] = jnp.broadcast_to(scale / total, (LANES, LANES)).T

            for half, out in enumerate((kept, sent)):
                out[pair, 0:4, :] = rows[pair][0:4, half * slab : (half + 1) * slab]
                for start in range(0, slab, LANES):
                    lanes = slice(half * slab + start, half * slab + start + LANES)
                    mutual = jnp.zeros((64, LANES), jnp.float32)
                    for row in range(0, tokens, 64):
                        mutual += products[pair][row : row + 64, lanes] * weights[row : row + 64, :]
                    out[pair, 4:5, start : start + LANES] = jnp.sum(mutual, axis=0, keepdims=True)


def mutual(meta, products, rows, columns, others):
    pairs = len(products)
    tokens = products[0].shape[0]
    shape = jax.ShapeDtypeStruct((pairs, 8, tokens // 2), jnp.float32)
    return pl.pallas_call(
        functools.partial(mutual_kernel, pairs),
        in_specs=[SMEM] + [VMEM] * (2 * pairs + 2),
        out_specs=[VMEM] * 2,
        out_shape=[shape] * 2,
        scratch_shapes=[pltpu.VMEM((tokens, LANES), jnp.float32)],
        compiler_params=pltpu.CompilerParams(vmem_limit_bytes=20 * 1024 * 1024),
    )(meta, *products, *rows, columns, others)


def shards(picture_descriptors, image_slot, group_images, pair_target, pair_count):
    chips = lax.axis_size("chip")
    cores = lax.axis_size("core")
    quads = lax.axis_size("quad")
    groups = chips * cores
    chip = lax.axis_index("chip").astype(jnp.int32)
    core = lax.axis_index("core").astype(jnp.int32)
    quad = lax.axis_index("quad").astype(jnp.int32)
    images_dev, slab, width = picture_descriptors.shape
    pairs = pair_target.shape[0]
    chip_rows = images_dev * cores
    image_rows = slab * quads // IMG_W
    multiplier = 1.0 / (width * SHARPNESS_DIVISOR)

    def all_pairs(array):
        return lax.all_to_all(array, ("chip", "core"), split_axis=0, concat_axis=0, tiled=True)

    traded = lax.ppermute(picture_descriptors, "core", [(i, (i + 1) % cores) for i in range(cores)])

    asked = all_pairs(announce(groups, image_slot, group_images, pair_target, pair_count))

    capacities = [size for size in CAPACITIES if size < chip_rows] + [chip_rows]
    asked = asked.reshape(groups, LANES)
    places, listed, branch = plan(chip_rows, 2 * pairs, capacities, chip[None], asked)
    halves = (images_dev, cores, chips, slab // groups, width)

    def exchange(capacity, operands):
        own, other, rows, places, asked = operands
        pieces = pick(capacity, core[None], rows, own, other)
        spread = lax.all_to_all(pieces, "chip", split_axis=0, concat_axis=0, tiled=True)
        return regroup(groups, 2 * pairs, locate(chip_rows, 2 * pairs, places, asked), spread)

    pieces = lax.switch(
        branch[0],
        [functools.partial(exchange, size) for size in capacities],
        (picture_descriptors.reshape(halves), traded.reshape(halves), listed, places, asked),
    )
    maps = all_pairs(pieces).reshape(chips, cores, *pieces.shape[1:])

    def trade(array, flip):
        return lax.ppermute(array, "quad", [(i, i ^ flip) for i in range(quads)])

    query_flip, target_flip = 1, quads - 1
    meta = jnp.stack([quad, pair_count[0], quad, quad ^ target_flip])
    products, rows, columns = [], [], ()
    for pair in range(pairs):
        near_query = trade(maps[:, :, pair : pair + 1], query_flip)
        near_target = trade(maps[:, :, pairs + pair : pairs + pair + 1], target_flip)
        if pair < pairs - 1:
            product, row, column = score(image_rows, multiplier, pair, meta, maps, near_query, near_target, columns)
        else:
            scores, powers, column = score_columns(multiplier, pair, meta, maps, near_query, near_target, columns)
            others = trade(column, target_flip)
            product, row = score_rows(image_rows, pair, meta, scores, powers)
        products.append(product)
        rows.append(row)
        columns = (column,)
    kept, sent = mutual(meta, products, rows, columns[0], others)
    partial = jnp.stack([kept, trade(sent, query_flip)])
    top = partial[:, :, 0]
    weight = jnp.exp(top - jnp.max(top, axis=0, keepdims=True))
    total = jnp.sum(partial[:, :, 1] * weight, axis=0)
    fields = [jnp.sum(partial[:, :, 2 + field] * weight, axis=0) / total for field in range(3)]
    in_use = jnp.arange(pairs, dtype=jnp.int32) < pair_count[0]
    return jnp.where(in_use[None, :, None], jnp.stack(fields), 0.0).transpose(1, 0, 2)


def solution(mesh):
    pair_axis = ("chip", "core")
    split = Mesh(mesh.devices.reshape(-1, CORES, mesh.devices.shape[-1]), (*pair_axis, "quad"))
    return jax.shard_map(
        shards,
        mesh=split,
        in_specs=(P(pair_axis, "quad", None), P(), P(pair_axis), P(pair_axis), P(pair_axis)),
        out_specs=P(pair_axis, None, "quad"),
        check_vma=False,
    )
```

profile of v0, /device:TPU:40, one launch (start us, length us, event | category | flops | bytes accessed | tf_op | source)
XLA Modules:
  0.0 124.1 jit_solution(14854979691031550444)
XLA Ops:
  0.0 0.0 collective-permute-start
  0.7 1.4 %shard_map.55 = s32[64,1,128]{2,1,0:T(1,128)} custom-call(s32[1024]{0:T(1024)} %image_slot.1, s32[10]{0:T(128)} %group_images.1, s32[2]{0:T(128)} %pair_target.1, s32[1]{0:T(128)} %copy.59.pair_count), custom_call_target="tpu_custom_call" | custom-call | tf_op jit(solution)/shard_map/pallas_call | solution.py:36
  2.0 11.8 %all-to-all-start.9 = ((s32[64,1,128]{2,1,0:T(1,128)}), s32[64,1,128]{2,1,0:T(1,128)S(1)}, u32[]{:S(2)}, u32[]{:S(2)}) async-start(s32[64,1,128]{2,1,0:T(1,128)} %shard_map.55), calls=%async_computation.9 | async-start | bytes 65536 | tf_op jit(solution)/shard_map/all_to_all | solution.py:411
  13.8 7.7 %all-to-all-done.9 = s32[64,1,128]{2,1,0:T(1,128)S(1)} async-done(((s32[64,1,128]{2,1,0:T(1,128)}), s32[64,1,128]{2,1,0:T(1,128)S(1)}, u32[]{:S(2)}, u32[]{:S(2)}) %all-to-all-start.9) | async-done | bytes 32800 | tf_op jit(solution)/shard_map/all_to_all | solution.py:411
  21.5 1.0 shard_map.56
  23.1 0.0 collective-permute-done
  23.1 38.5 %conditional.1 = (bf16[64,4,8,256]{3,2,1,0:T(8,128)(2,1)S(1)}) conditional(s32[]{:T(128)} %bitcast.14, (f32[32,32]{1,0:T(8,128)S(1)}, s32[64,128]{1,0:T(8,128)S(1)}, s32[]{:T(128)}, s32[8,128]{1,0:T(8,128)S(1)}, bf16[16,2,32,8,256]{4,3,2,1,0:T(8,128)(2,1)}, ...), branch_computations={%region_0.0_spmd, %region_1.0_spmd, %region_2.0_spmd, %region_3.0_... | conditional | bytes 29368416 | solution.py:428
  23.1 3.0 %branch_2_fun.4 = bf16[32,8,8,256]{3,2,1,0:T(8,128)(2,1)} custom-call(s32[1]{0:T(128)} %bitcast.2.core, s32[8,128]{1,0:T(8,128)S(1)} %get-tuple-element.138.rows, bf16[16,2,32,8,256]{4,3,2,1,0:T(8,128)(2,1)} %get-tuple-element.139.own, bf16[16,2,32,8,256]{4,3,2,1,0:T(8,128)(2,1)} %get-tuple-element.140.other), custom_call_target="tpu_custom_call" | custom-call | tf_op jit(solution)/shard_map/cond/branch_2_fun/pallas_call | solution.py:137
  26.1 5.9 %all-to-all-start.2 = ((bf16[32,8,8,256]{3,2,1,0:T(8,128)(2,1)}), bf16[32,8,8,256]{3,2,1,0:T(8,128)(2,1)S(1)}, u32[]{:S(2)}, u32[]{:S(2)}) async-start(bf16[32,8,8,256]{3,2,1,0:T(8,128)(2,1)} %branch_2_fun.4), calls=%async_computation.2 | async-start | bytes 2097152 | tf_op jit(solution)/shard_map/cond/branch_2_fun/all_to_all | solution.py:425
  32.0 0.8 branch_2_fun.3.index
  32.8 26.7 %all-to-all-done.2.spread = bf16[32,8,8,256]{3,2,1,0:T(8,128)(2,1)S(1)} async-done(((bf16[32,8,8,256]{3,2,1,0:T(8,128)(2,1)}), bf16[32,8,8,256]{3,2,1,0:T(8,128)(2,1)S(1)}, u32[]{:S(2)}, u32[]{:S(2)}) %all-to-all-start.2) | async-done | bytes 1048608 | tf_op jit(solution)/shard_map/cond/branch_2_fun/all_to_all | solution.py:425
  59.6 0.0 copy-start.3
  59.6 0.7 copy-done.3
  60.3 1.3 %branch_2_fun.5 = bf16[64,4,8,256]{3,2,1,0:T(8,128)(2,1)S(1)} custom-call(s32[8,64]{1,0:T(8,128)S(1)} %copy-done.3, bf16[32,8,8,256]{3,2,1,0:T(8,128)(2,1)S(1)} %all-to-all-done.2.spread), custom_call_target="tpu_custom_call" | custom-call | tf_op jit(solution)/shard_map/cond/branch_2_fun/pallas_call | solution.py:160
  61.6 34.6 %all_to_all.46 = bf16[64,4,8,256]{3,2,1,0:T(8,128)(2,1)S(1)} all-to-all(bf16[64,4,8,256]{3,2,1,0:T(8,128)(2,1)S(1)} %get-tuple-element.222), channel_id=1, replica_groups=mesh['chip'=32,'core'=2,'quad'=4] {'chip','core'}, dimensions={0} | all-to-all | bytes 2097152 | tf_op jit(solution)/shard_map/all_to_all | solution.py:411
  96.2 0.1 fusion.11
  96.3 2.8 %collective-permute-start.2 = (bf16[32,2,1,8,256]{4,3,2,1,0:T(8,128)(2,1)S(1)}, bf16[32,2,1,8,256]{4,3,2,1,0:T(8,128)(2,1)S(1)}, u32[]{:S(2)}, u32[]{:S(2)}) collective-permute-start(bf16[32,2,1,8,256]{4,3,2,1,0:T(8,128)(2,1)S(1)} %get-tuple-element.211), channel_id=1, source_target_pairs={{0,3},{1,2},{2,1},{3,0},{4,7},{5,6},{6,5},{7,4},{8,11},{9,10},{10,... | collective-permute-start | bytes 786440 | tf_op jit(solution)/shard_map/ppermute | solution.py:436
  99.1 0.2 collective-permute-start.1
  99.3 1.1 collective-permute-start.4
  100.5 0.7 collective-permute-start.3
  101.1 0.1 pad_add_fusion.meta
  101.2 5.6 %collective-permute-done.2.near_target = bf16[32,2,1,8,256]{4,3,2,1,0:T(8,128)(2,1)S(1)} collective-permute-done((bf16[32,2,1,8,256]{4,3,2,1,0:T(8,128)(2,1)S(1)}, bf16[32,2,1,8,256]{4,3,2,1,0:T(8,128)(2,1)S(1)}, u32[]{:S(2)}, u32[]{:S(2)}) %collective-permute-start.2) | collective-permute-done | bytes 262176 | tf_op jit(solution)/shard_map/ppermute | solution.py:436
  106.8 1.6 %collective-permute-done.1.near_query = bf16[32,2,1,8,256]{4,3,2,1,0:T(8,128)(2,1)S(1)} collective-permute-done((bf16[32,2,1,8,256]{4,3,2,1,0:T(8,128)(2,1)S(1)}, bf16[32,2,1,8,256]{4,3,2,1,0:T(8,128)(2,1)S(1)}, u32[]{:S(2)}, u32[]{:S(2)}) %collective-permute-start.1) | collective-permute-done | bytes 262176 | tf_op jit(solution)/shard_map/ppermute | solution.py:436
  108.4 3.3 %shard_map.57 = (f32[1024,1024]{1,0:T(8,128)S(1)}, f32[8,1024]{1,0:T(8,128)S(1)}, f32[1,8,1024]{2,1,0:T(8,128)S(1)}) custom-call(s32[4]{0:T(128)S(1)} %pad_add_fusion.meta, bf16[32,2,4,8,256]{4,3,2,1,0:T(8,128)(2,1)S(1)} %bitcast.66, bf16[32,2,1,8,256]{4,3,2,1,0:T(8,128)(2,1)S(1)} %collective-permute-done.1.near_query, ...), custom_call_target="tpu_custom_call" | custom-call | flops 536870912 | bytes 2097152 | tf_op jit(solution)/shard_map/pallas_call | solution.py:239
  111.6 0.0 collective-permute-done.4.near_target
  111.6 0.6 collective-permute-done.3.near_query
  112.2 0.5 shard_map.58
  112.7 1.6 %collective-permute-start.5 = (f32[2,8,1024]{2,1,0:T(8,128)S(1)}, f32[2,8,1024]{2,1,0:T(8,128)S(1)}, u32[]{:S(2)}, u32[]{:S(2)}) collective-permute-start(f32[2,8,1024]{2,1,0:T(8,128)S(1)} %get-tuple-element.200.refs_4_), channel_id=1, source_target_pairs={{0,3},{1,2},{2,1},{3,0},{4,7},{5,6},{6,5},{7,4},{8,11},{9,10},{10,... | collective-permute-start | bytes 196616 | tf_op jit(solution)/shard_map/ppermute | solution.py:436
  114.3 0.5 shard_map.59
  114.9 3.4 %collective-permute-done.5.refs_5_ = f32[2,8,1024]{2,1,0:T(8,128)S(1)} collective-permute-done((f32[2,8,1024]{2,1,0:T(8,128)S(1)}, f32[2,8,1024]{2,1,0:T(8,128)S(1)}, u32[]{:S(2)}, u32[]{:S(2)}) %collective-permute-start.5) | collective-permute-done | bytes 65568 | tf_op jit(solution)/shard_map/ppermute | solution.py:436
  118.3 1.0 shard_map.60
  119.3 0.1 collective-permute-start.6
  119.4 3.9 %collective-permute-done.6 = f32[2,8,512]{2,1,0:T(8,128)S(1)} collective-permute-done((f32[2,8,512]{2,1,0:T(8,128)S(1)}, f32[2,8,512]{2,1,0:T(8,128)S(1)}, u32[]{:S(2)}, u32[]{:S(2)}) %collective-permute-start.6) | collective-permute-done | bytes 32800 | tf_op jit(solution)/shard_map/ppermute | solution.py:436
  123.4 0.7 fusion
  (4 shorter events, 0.1 us)
Async XLA Ops:
  0.0 23.1 %collective-permute-start = (bf16[16,512,256]{2,1,0:T(8,128)(2,1)}, bf16[16,512,256]{2,1,0:T(8,128)(2,1)}, u32[]{:S(2)}, u32[]{:S(2)}) collective-permute-start(bf16[16,512,256]{2,1,0:T(8,128)(2,1)} %param.14), channel_id=1, source_target_pairs={{0,4},{4,0},{1,5},{5,1},{2,6},{6,2},{3,7},{7,3},{8,12},{12,8},{9,1... | collective-permute-start | bytes 12582920 | tf_op jit(solution)/shard_map/ppermute | solution.py:413
  2.0 19.5 %all-to-all-start.9 = ((s32[64,1,128]{2,1,0:T(1,128)}), s32[64,1,128]{2,1,0:T(1,128)S(1)}, u32[]{:S(2)}, u32[]{:S(2)}) async-start(s32[64,1,128]{2,1,0:T(1,128)} %shard_map.55), calls=%async_computation.9 | async-start | bytes 65536 | tf_op jit(solution)/shard_map/all_to_all | solution.py:411
  26.1 33.5 %all-to-all-start.2 = ((bf16[32,8,8,256]{3,2,1,0:T(8,128)(2,1)}), bf16[32,8,8,256]{3,2,1,0:T(8,128)(2,1)S(1)}, u32[]{:S(2)}, u32[]{:S(2)}) async-start(bf16[32,8,8,256]{3,2,1,0:T(8,128)(2,1)} %branch_2_fun.4), calls=%async_computation.2 | async-start | bytes 2097152 | tf_op jit(solution)/shard_map/cond/branch_2_fun/all_to_all | solution.py:425
  59.6 0.7 copy-start.3
  96.3 10.5 %collective-permute-start.2 = (bf16[32,2,1,8,256]{4,3,2,1,0:T(8,128)(2,1)S(1)}, bf16[32,2,1,8,256]{4,3,2,1,0:T(8,128)(2,1)S(1)}, u32[]{:S(2)}, u32[]{:S(2)}) collective-permute-start(bf16[32,2,1,8,256]{4,3,2,1,0:T(8,128)(2,1)S(1)} %get-tuple-element.211), channel_id=1, source_target_pairs={{0,3},{1,2},{2,1},{3,0},{4,7},{5,6},{6,5},{7,4},{8,11},{9,10},{10,... | collective-permute-start | bytes 786440 | tf_op jit(solution)/shard_map/ppermute | solution.py:436
  99.1 9.2 %collective-permute-start.1 = (bf16[32,2,1,8,256]{4,3,2,1,0:T(8,128)(2,1)S(1)}, bf16[32,2,1,8,256]{4,3,2,1,0:T(8,128)(2,1)S(1)}, u32[]{:S(2)}, u32[]{:S(2)}) collective-permute-start(bf16[32,2,1,8,256]{4,3,2,1,0:T(8,128)(2,1)S(1)} %get-tuple-element.212), channel_id=1, source_target_pairs={{0,1},{1,0},{2,3},{3,2},{4,5},{5,4},{6,7},{7,6},{8,9},{9,8},{10,11... | collective-permute-start | bytes 786440 | tf_op jit(solution)/shard_map/ppermute | solution.py:436
  99.3 12.3 %collective-permute-start.4 = (bf16[32,2,1,8,256]{4,3,2,1,0:T(8,128)(2,1)S(1)}, bf16[32,2,1,8,256]{4,3,2,1,0:T(8,128)(2,1)S(1)}, u32[]{:S(2)}, u32[]{:S(2)}) collective-permute-start(bf16[32,2,1,8,256]{4,3,2,1,0:T(8,128)(2,1)S(1)} %get-tuple-element.209), channel_id=1, source_target_pairs={{0,3},{1,2},{2,1},{3,0},{4,7},{5,6},{6,5},{7,4},{8,11},{9,10},{10,... | collective-permute-start | bytes 786440 | tf_op jit(solution)/shard_map/ppermute | solution.py:436
  100.5 11.7 %collective-permute-start.3 = (bf16[32,2,1,8,256]{4,3,2,1,0:T(8,128)(2,1)S(1)}, bf16[32,2,1,8,256]{4,3,2,1,0:T(8,128)(2,1)S(1)}, u32[]{:S(2)}, u32[]{:S(2)}) collective-permute-start(bf16[32,2,1,8,256]{4,3,2,1,0:T(8,128)(2,1)S(1)} %get-tuple-element.210), channel_id=1, source_target_pairs={{0,1},{1,0},{2,3},{3,2},{4,5},{5,4},{6,7},{7,6},{8,9},{9,8},{10,11... | collective-permute-start | bytes 786440 | tf_op jit(solution)/shard_map/ppermute | solution.py:436
  112.7 5.6 %collective-permute-start.5 = (f32[2,8,1024]{2,1,0:T(8,128)S(1)}, f32[2,8,1024]{2,1,0:T(8,128)S(1)}, u32[]{:S(2)}, u32[]{:S(2)}) collective-permute-start(f32[2,8,1024]{2,1,0:T(8,128)S(1)} %get-tuple-element.200.refs_4_), channel_id=1, source_target_pairs={{0,3},{1,2},{2,1},{3,0},{4,7},{5,6},{6,5},{7,4},{8,11},{9,10},{10,... | collective-permute-start | bytes 196616 | tf_op jit(solution)/shard_map/ppermute | solution.py:436
  119.3 4.0 %collective-permute-start.6 = (f32[2,8,512]{2,1,0:T(8,128)S(1)}, f32[2,8,512]{2,1,0:T(8,128)S(1)}, u32[]{:S(2)}, u32[]{:S(2)}) collective-permute-start(f32[2,8,512]{2,1,0:T(8,128)S(1)} %get-tuple-element.202), channel_id=1, source_target_pairs={{0,1},{1,0},{2,3},{3,2},{4,5},{5,4},{6,7},{7,6},{8,9},{9,8},{10,11... | collective-permute-start | bytes 98312 | tf_op jit(solution)/shard_map/ppermute | solution.py:436
where the time goes:
time: 126 us; the launch traced here: 124 us
  waiting for transfers between devices  49.5 us (39%)
  blocking collectives  34.6 us (27%)
  starting transfers between devices  24.3 us (19%)
  Pallas kernels  12.8 us (10%)
  between operations  1.31 us (1%)
    all_to_all x1, blocking collectives, all_pairs(): lax.all_to_all(array, ('chip', 'core'), split_axis=0, concat_axis=0, tile...  34.6 us
    all_to_all x1, waiting for transfers between devices, exchange(): lax.all_to_all(pieces, 'chip', split_axis=0, concat_axis=0, tiled=True)  26.7 us
    ppermute x6, waiting for transfers between devices, trade(): return lax.ppermute(array, 'quad', [(i, i ^ flip) for i in range(quads)])  15 us
    all_to_all x1, starting transfers between devices, all_pairs(): lax.all_to_all(array, ('chip', 'core'), split_axis=0, concat_axis=0, tile...  11.8 us
    all_to_all x1, waiting for transfers between devices, all_pairs(): lax.all_to_all(array, ('chip', 'core'), split_axis=0, concat_axis=0, tile...  7.72 us
    ppermute x6, starting transfers between devices, trade(): return lax.ppermute(array, 'quad', [(i, i ^ flip) for i in range(quads)])  6.55 us
    all_to_all x1, starting transfers between devices, exchange(): lax.all_to_all(pieces, 'chip', split_axis=0, concat_axis=0, tiled=True)  5.94 us
    pallas_call x1, Pallas kernels, score(): pl.pallas_call(functools.partial(score_kernel, image_rows, multiplier, pa...  3.25 us
  transfers between devices with their start and end apart: 9, of which 7 were waited for; matrix products, arithmetic and copies ran while one was open for 0% of the time, Pallas kernels for 6%

commit v1 on v0

--- a/solution.py
+++ b/solution.py
@@ -144,8 +144,11 @@
     )(core, rows, own, other)
 
 
-def regroup_kernel(index, spread, out):
+def regroup_kernel(located, spread, out, index, sem):
     groups, entries = out.shape[:2]
+    copy = pltpu.make_async_copy(located, index, sem)
+    copy.start()
+    copy.wait()
 
     def step(group, carry):
         for entry in range(entries):
@@ -159,9 +162,10 @@
 def regroup(groups, entries, index, spread):
     return pl.pallas_call(
         regroup_kernel,
-        in_specs=[SMEM, VMEM],
+        in_specs=[ANY, VMEM],
         out_specs=VMEM,
         out_shape=jax.ShapeDtypeStruct((groups, entries, *spread.shape[2:]), spread.dtype),
+        scratch_shapes=[pltpu.SMEM(index.shape, jnp.int32), pltpu.SemaphoreType.DMA(())],
         compiler_params=pltpu.CompilerParams(vmem_limit_bytes=24 * 1024 * 1024),
     )(index, spread)
 

time: 126 us -> 125 us (level)
  no operation moved by 1% of the time
where the time goes in v1:
time: 125 us; the launch traced here: 124 us
  waiting for transfers between devices  49.5 us (40%)
  blocking collectives  34.6 us (28%)
  starting transfers between devices  24.3 us (19%)
  Pallas kernels  12.8 us (10%)
  between operations  1.31 us (1%)
    all_to_all x1, blocking collectives, all_pairs(): lax.all_to_all(array, ('chip', 'core'), split_axis=0, concat_axis=0, tile...  34.6 us
    all_to_all x1, waiting for transfers between devices, exchange(): lax.all_to_all(pieces, 'chip', split_axis=0, concat_axis=0, tiled=True)  26.7 us
    ppermute x6, waiting for transfers between devices, trade(): return lax.ppermute(array, 'quad', [(i, i ^ flip) for i in range(quads)])  15 us
    all_to_all x1, starting transfers between devices, all_pairs(): lax.all_to_all(array, ('chip', 'core'), split_axis=0, concat_axis=0, tile...  11.8 us
    all_to_all x1, waiting for transfers between devices, all_pairs(): lax.all_to_all(array, ('chip', 'core'), split_axis=0, concat_axis=0, tile...  7.72 us
    ppermute x6, starting transfers between devices, trade(): return lax.ppermute(array, 'quad', [(i, i ^ flip) for i in range(quads)])  6.55 us
    all_to_all x1, starting transfers between devices, exchange(): lax.all_to_all(pieces, 'chip', split_axis=0, concat_axis=0, tiled=True)  5.94 us
    pallas_call x1, Pallas kernels, score(): pl.pallas_call(functools.partial(score_kernel, image_rows, multiplier, pa...  3.25 us
  transfers between devices with their start and end apart: 9, of which 7 were waited for; matrix products, arithmetic and copies ran while one was open for 0% of the time, Pallas kernels for 6%

profile of v1, /device:TPU:40, one launch (start us, length us, event | category | flops | bytes accessed | tf_op | source)
XLA Modules:
  0.0 124.1 jit_solution(10248938549125816158)
XLA Ops:
  0.0 0.0 collective-permute-start
  0.7 1.4 %shard_map.55 = s32[64,1,128]{2,1,0:T(1,128)} custom-call(s32[1024]{0:T(1024)} %image_slot.1, s32[10]{0:T(128)} %group_images.1, s32[2]{0:T(128)} %pair_target.1, s32[1]{0:T(128)} %copy.59.pair_count), custom_call_target="tpu_custom_call" | custom-call | tf_op jit(solution)/shard_map/pallas_call | solution.py:36
  2.0 11.8 %all-to-all-start.9 = ((s32[64,1,128]{2,1,0:T(1,128)}), s32[64,1,128]{2,1,0:T(1,128)S(1)}, u32[]{:S(2)}, u32[]{:S(2)}) async-start(s32[64,1,128]{2,1,0:T(1,128)} %shard_map.55), calls=%async_computation.9 | async-start | bytes 65536 | tf_op jit(solution)/shard_map/all_to_all | solution.py:415
  13.8 7.7 %all-to-all-done.9 = s32[64,1,128]{2,1,0:T(1,128)S(1)} async-done(((s32[64,1,128]{2,1,0:T(1,128)}), s32[64,1,128]{2,1,0:T(1,128)S(1)}, u32[]{:S(2)}, u32[]{:S(2)}) %all-to-all-start.9) | async-done | bytes 32800 | tf_op jit(solution)/shard_map/all_to_all | solution.py:415
  21.5 1.0 shard_map.56
  23.1 0.0 collective-permute-done
  23.1 38.6 %conditional.1 = (bf16[64,4,8,256]{3,2,1,0:T(8,128)(2,1)S(1)}) conditional(s32[]{:T(128)} %bitcast.14, (f32[32,32]{1,0:T(8,128)S(1)}, s32[64,128]{1,0:T(8,128)S(1)}, s32[]{:T(128)}, s32[8,128]{1,0:T(8,128)S(1)}, bf16[16,2,32,8,256]{4,3,2,1,0:T(8,128)(2,1)}, ...), branch_computations={%region_0.0_spmd, %region_1.0_spmd, %region_2.0_spmd, %region_3.0_... | conditional | bytes 29368416 | solution.py:432
  23.1 3.0 %branch_2_fun.4 = bf16[32,8,8,256]{3,2,1,0:T(8,128)(2,1)} custom-call(s32[1]{0:T(128)} %bitcast.2.core, s32[8,128]{1,0:T(8,128)S(1)} %get-tuple-element.138.rows, bf16[16,2,32,8,256]{4,3,2,1,0:T(8,128)(2,1)} %get-tuple-element.139.own, bf16[16,2,32,8,256]{4,3,2,1,0:T(8,128)(2,1)} %get-tuple-element.140.other), custom_call_target="tpu_custom_call" | custom-call | tf_op jit(solution)/shard_map/cond/branch_2_fun/pallas_call | solution.py:137
  26.1 5.9 %all-to-all-start.2 = ((bf16[32,8,8,256]{3,2,1,0:T(8,128)(2,1)}), bf16[32,8,8,256]{3,2,1,0:T(8,128)(2,1)S(1)}, u32[]{:S(2)}, u32[]{:S(2)}) async-start(bf16[32,8,8,256]{3,2,1,0:T(8,128)(2,1)} %branch_2_fun.4), calls=%async_computation.2 | async-start | bytes 2097152 | tf_op jit(solution)/shard_map/cond/branch_2_fun/all_to_all | solution.py:429
  32.0 0.8 branch_2_fun.3.located
  32.8 26.7 %all-to-all-done.2.spread = bf16[32,8,8,256]{3,2,1,0:T(8,128)(2,1)S(1)} async-done(((bf16[32,8,8,256]{3,2,1,0:T(8,128)(2,1)}), bf16[32,8,8,256]{3,2,1,0:T(8,128)(2,1)S(1)}, u32[]{:S(2)}, u32[]{:S(2)}) %all-to-all-start.2) | async-done | bytes 1048608 | tf_op jit(solution)/shard_map/cond/branch_2_fun/all_to_all | solution.py:429
  59.6 0.0 copy-start.3
  59.6 0.7 copy-done.3
  60.3 1.3 %branch_2_fun.5 = bf16[64,4,8,256]{3,2,1,0:T(8,128)(2,1)S(1)} custom-call(s32[8,64]{1,0:T(8,128)S(1)} %copy-done.3, bf16[32,8,8,256]{3,2,1,0:T(8,128)(2,1)S(1)} %all-to-all-done.2.spread), custom_call_target="tpu_custom_call" | custom-call | tf_op jit(solution)/shard_map/cond/branch_2_fun/pallas_call | solution.py:163
  61.6 34.6 %all_to_all.46 = bf16[64,4,8,256]{3,2,1,0:T(8,128)(2,1)S(1)} all-to-all(bf16[64,4,8,256]{3,2,1,0:T(8,128)(2,1)S(1)} %get-tuple-element.222), channel_id=1, replica_groups=mesh['chip'=32,'core'=2,'quad'=4] {'chip','core'}, dimensions={0} | all-to-all | bytes 2097152 | tf_op jit(solution)/shard_map/all_to_all | solution.py:415
  96.2 0.1 fusion.11
  96.3 2.8 %collective-permute-start.2 = (bf16[32,2,1,8,256]{4,3,2,1,0:T(8,128)(2,1)S(1)}, bf16[32,2,1,8,256]{4,3,2,1,0:T(8,128)(2,1)S(1)}, u32[]{:S(2)}, u32[]{:S(2)}) collective-permute-start(bf16[32,2,1,8,256]{4,3,2,1,0:T(8,128)(2,1)S(1)} %get-tuple-element.211), channel_id=1, source_target_pairs={{0,3},{1,2},{2,1},{3,0},{4,7},{5,6},{6,5},{7,4},{8,11},{9,10},{10,... | collective-permute-start | bytes 786440 | tf_op jit(solution)/shard_map/ppermute | solution.py:440
  99.1 0.2 collective-permute-start.1
  99.4 1.1 collective-permute-start.4
  100.5 0.7 collective-permute-start.3
  101.2 0.1 pad_add_fusion.meta
  101.2 5.6 %collective-permute-done.2.near_target = bf16[32,2,1,8,256]{4,3,2,1,0:T(8,128)(2,1)S(1)} collective-permute-done((bf16[32,2,1,8,256]{4,3,2,1,0:T(8,128)(2,1)S(1)}, bf16[32,2,1,8,256]{4,3,2,1,0:T(8,128)(2,1)S(1)}, u32[]{:S(2)}, u32[]{:S(2)}) %collective-permute-start.2) | collective-permute-done | bytes 262176 | tf_op jit(solution)/shard_map/ppermute | solution.py:440
  106.8 1.6 %collective-permute-done.1.near_query = bf16[32,2,1,8,256]{4,3,2,1,0:T(8,128)(2,1)S(1)} collective-permute-done((bf16[32,2,1,8,256]{4,3,2,1,0:T(8,128)(2,1)S(1)}, bf16[32,2,1,8,256]{4,3,2,1,0:T(8,128)(2,1)S(1)}, u32[]{:S(2)}, u32[]{:S(2)}) %collective-permute-start.1) | collective-permute-done | bytes 262176 | tf_op jit(solution)/shard_map/ppermute | solution.py:440
  108.4 3.3 %shard_map.57 = (f32[1024,1024]{1,0:T(8,128)S(1)}, f32[8,1024]{1,0:T(8,128)S(1)}, f32[1,8,1024]{2,1,0:T(8,128)S(1)}) custom-call(s32[4]{0:T(128)S(1)} %pad_add_fusion.meta, bf16[32,2,4,8,256]{4,3,2,1,0:T(8,128)(2,1)S(1)} %bitcast.66, bf16[32,2,1,8,256]{4,3,2,1,0:T(8,128)(2,1)S(1)} %collective-permute-done.1.near_query, ...), custom_call_target="tpu_custom_call" | custom-call | flops 536870912 | bytes 2097152 | tf_op jit(solution)/shard_map/pallas_call | solution.py:243
  111.6 0.0 collective-permute-done.4.near_target
  111.6 0.6 collective-permute-done.3.near_query
  112.2 0.5 shard_map.58
  112.8 1.6 %collective-permute-start.5 = (f32[2,8,1024]{2,1,0:T(8,128)S(1)}, f32[2,8,1024]{2,1,0:T(8,128)S(1)}, u32[]{:S(2)}, u32[]{:S(2)}) collective-permute-start(f32[2,8,1024]{2,1,0:T(8,128)S(1)} %get-tuple-element.200.refs_4_), channel_id=1, source_target_pairs={{0,3},{1,2},{2,1},{3,0},{4,7},{5,6},{6,5},{7,4},{8,11},{9,10},{10,... | collective-permute-start | bytes 196616 | tf_op jit(solution)/shard_map/ppermute | solution.py:440
  114.3 0.5 shard_map.59
  114.9 3.4 %collective-permute-done.5.refs_5_ = f32[2,8,1024]{2,1,0:T(8,128)S(1)} collective-permute-done((f32[2,8,1024]{2,1,0:T(8,128)S(1)}, f32[2,8,1024]{2,1,0:T(8,128)S(1)}, u32[]{:S(2)}, u32[]{:S(2)}) %collective-permute-start.5) | collective-permute-done | bytes 65568 | tf_op jit(solution)/shard_map/ppermute | solution.py:440
  118.3 1.0 shard_map.60
  119.3 0.1 collective-permute-start.6
  119.4 3.9 %collective-permute-done.6 = f32[2,8,512]{2,1,0:T(8,128)S(1)} collective-permute-done((f32[2,8,512]{2,1,0:T(8,128)S(1)}, f32[2,8,512]{2,1,0:T(8,128)S(1)}, u32[]{:S(2)}, u32[]{:S(2)}) %collective-permute-start.6) | collective-permute-done | bytes 32800 | tf_op jit(solution)/shard_map/ppermute | solution.py:440
  123.4 0.7 fusion
  (4 shorter events, 0.1 us)
Async XLA Ops:
  0.0 23.1 %collective-permute-start = (bf16[16,512,256]{2,1,0:T(8,128)(2,1)}, bf16[16,512,256]{2,1,0:T(8,128)(2,1)}, u32[]{:S(2)}, u32[]{:S(2)}) collective-permute-start(bf16[16,512,256]{2,1,0:T(8,128)(2,1)} %param.14), channel_id=1, source_target_pairs={{0,4},{4,0},{1,5},{5,1},{2,6},{6,2},{3,7},{7,3},{8,12},{12,8},{9,1... | collective-permute-start | bytes 12582920 | tf_op jit(solution)/shard_map/ppermute | solution.py:417
  2.0 19.5 %all-to-all-start.9 = ((s32[64,1,128]{2,1,0:T(1,128)}), s32[64,1,128]{2,1,0:T(1,128)S(1)}, u32[]{:S(2)}, u32[]{:S(2)}) async-start(s32[64,1,128]{2,1,0:T(1,128)} %shard_map.55), calls=%async_computation.9 | async-start | bytes 65536 | tf_op jit(solution)/shard_map/all_to_all | solution.py:415
  26.1 33.5 %all-to-all-start.2 = ((bf16[32,8,8,256]{3,2,1,0:T(8,128)(2,1)}), bf16[32,8,8,256]{3,2,1,0:T(8,128)(2,1)S(1)}, u32[]{:S(2)}, u32[]{:S(2)}) async-start(bf16[32,8,8,256]{3,2,1,0:T(8,128)(2,1)} %branch_2_fun.4), calls=%async_computation.2 | async-start | bytes 2097152 | tf_op jit(solution)/shard_map/cond/branch_2_fun/all_to_all | solution.py:429
  59.6 0.7 copy-start.3
  96.3 10.5 %collective-permute-start.2 = (bf16[32,2,1,8,256]{4,3,2,1,0:T(8,128)(2,1)S(1)}, bf16[32,2,1,8,256]{4,3,2,1,0:T(8,128)(2,1)S(1)}, u32[]{:S(2)}, u32[]{:S(2)}) collective-permute-start(bf16[32,2,1,8,256]{4,3,2,1,0:T(8,128)(2,1)S(1)} %get-tuple-element.211), channel_id=1, source_target_pairs={{0,3},{1,2},{2,1},{3,0},{4,7},{5,6},{6,5},{7,4},{8,11},{9,10},{10,... | collective-permute-start | bytes 786440 | tf_op jit(solution)/shard_map/ppermute | solution.py:440
  99.1 9.2 %collective-permute-start.1 = (bf16[32,2,1,8,256]{4,3,2,1,0:T(8,128)(2,1)S(1)}, bf16[32,2,1,8,256]{4,3,2,1,0:T(8,128)(2,1)S(1)}, u32[]{:S(2)}, u32[]{:S(2)}) collective-permute-start(bf16[32,2,1,8,256]{4,3,2,1,0:T(8,128)(2,1)S(1)} %get-tuple-element.212), channel_id=1, source_target_pairs={{0,1},{1,0},{2,3},{3,2},{4,5},{5,4},{6,7},{7,6},{8,9},{9,8},{10,11... | collective-permute-start | bytes 786440 | tf_op jit(solution)/shard_map/ppermute | solution.py:440
  99.4 12.3 %collective-permute-start.4 = (bf16[32,2,1,8,256]{4,3,2,1,0:T(8,128)(2,1)S(1)}, bf16[32,2,1,8,256]{4,3,2,1,0:T(8,128)(2,1)S(1)}, u32[]{:S(2)}, u32[]{:S(2)}) collective-permute-start(bf16[32,2,1,8,256]{4,3,2,1,0:T(8,128)(2,1)S(1)} %get-tuple-element.209), channel_id=1, source_target_pairs={{0,3},{1,2},{2,1},{3,0},{4,7},{5,6},{6,5},{7,4},{8,11},{9,10},{10,... | collective-permute-start | bytes 786440 | tf_op jit(solution)/shard_map/ppermute | solution.py:440
  100.5 11.7 %collective-permute-start.3 = (bf16[32,2,1,8,256]{4,3,2,1,0:T(8,128)(2,1)S(1)}, bf16[32,2,1,8,256]{4,3,2,1,0:T(8,128)(2,1)S(1)}, u32[]{:S(2)}, u32[]{:S(2)}) collective-permute-start(bf16[32,2,1,8,256]{4,3,2,1,0:T(8,128)(2,1)S(1)} %get-tuple-element.210), channel_id=1, source_target_pairs={{0,1},{1,0},{2,3},{3,2},{4,5},{5,4},{6,7},{7,6},{8,9},{9,8},{10,11... | collective-permute-start | bytes 786440 | tf_op jit(solution)/shard_map/ppermute | solution.py:440
  112.8 5.6 %collective-permute-start.5 = (f32[2,8,1024]{2,1,0:T(8,128)S(1)}, f32[2,8,1024]{2,1,0:T(8,128)S(1)}, u32[]{:S(2)}, u32[]{:S(2)}) collective-permute-start(f32[2,8,1024]{2,1,0:T(8,128)S(1)} %get-tuple-element.200.refs_4_), channel_id=1, source_target_pairs={{0,3},{1,2},{2,1},{3,0},{4,7},{5,6},{6,5},{7,4},{8,11},{9,10},{10,... | collective-permute-start | bytes 196616 | tf_op jit(solution)/shard_map/ppermute | solution.py:440
  119.3 4.0 %collective-permute-start.6 = (f32[2,8,512]{2,1,0:T(8,128)S(1)}, f32[2,8,512]{2,1,0:T(8,128)S(1)}, u32[]{:S(2)}, u32[]{:S(2)}) collective-permute-start(f32[2,8,512]{2,1,0:T(8,128)S(1)} %get-tuple-element.202), channel_id=1, source_target_pairs={{0,1},{1,0},{2,3},{3,2},{4,5},{5,4},{6,7},{7,6},{8,9},{9,8},{10,11... | collective-permute-start | bytes 98312 | tf_op jit(solution)/shard_map/ppermute | solution.py:440
